TPU v7x, 32 devices: a whole 2x2x4 slice. The times are simulated.
32 devices in a mesh: seq: 16 (over z, y, x), head: 2 (over core).
Axes of the slice: x: 2, y: 2, z: 4, core: 2. Of those that a mesh axis runs over, the one named last changes fastest.
Arguments:
- query_rows: bfloat16 [8192, 8, 128], P('seq', 'head'), may hold values from -8 to 8
- key_rows: bfloat16 [8192, 8, 128], P('seq', 'head'), may hold values from -8 to 8
- value_rows: bfloat16 [8192, 8, 128], P('seq', 'head'), may hold values from -8 to 8
- out_weight: bfloat16 [8, 128, 2048], P('head'), may hold values from -0.1875 to 0.1875
Outputs:
- layer_out: bfloat16 [8192, 2048], P('seq', 'head')
All inputs are finite; a program needn't handle non-finite values.
Results may differ from a plain program's by a relative error of at most 0.015.
Values may be sent and summed in bfloat16 or wider, within the bound.
A program may use at most 64 MiB of HBM per device.

v0:
```python
import jax
import jax.numpy as jnp
from jax import lax
from jax.sharding import PartitionSpec as P

BLOCK = 128


def partner_2(value, axis, distance):
    mask = 2**distance
    pairs = [(source, source ^ mask) for source in range(lax.axis_size(axis))]
    return lax.ppermute(value, axis, pairs)


def with_halo(value, sides, width):
    for axis, dim in sides:
        size, length = (lax.axis_size(axis), value.shape[dim])
        up = [(i, (i + 1) % size) for i in range(size - 1)]
        down = [(j, i) for i, j in up]
        last = lax.slice_in_dim(value, length - width, length, axis=dim)
        initial = lax.slice_in_dim(value, 0, width, axis=dim)
        before = lax.ppermute(last, axis, up)
        after = lax.ppermute(initial, axis, down)
        value = jnp.concatenate([before, value, after], axis=dim)
    return value


def shifted(value, axis, steps):
    count = lax.axis_size(axis)
    initial, last = (max(0, -steps), min(count, count - steps))
    return lax.ppermute(value, axis, [(source, source + steps) for source in range(initial, last)])


def coarsen(source, level_index, average):
    count = source.shape[0] >> level_index
    grouped = source.astype(jnp.float32).reshape((count, 1 << level_index) + source.shape[1:])
    summed = jnp.sum(grouped, axis=1)
    if average:
        summed = summed / float(1 << level_index)
    return summed.astype(jnp.bfloat16)


def slot_targets(block_index, level_index):
    if level_index == 0:
        return [block_index - 1, block_index, block_index + 1]
    return [
        block_index - 2,
        block_index + 2,
        jnp.where(block_index % 2 == 0, block_index + 3, block_index - 3),
    ]


def slot_masks(block_index, block_total, level_index, width):
    targets = slot_targets(block_index, level_index)
    return jnp.concatenate(
        [
            jnp.repeat(((target >= 0) & (target < block_total))[:, None], width, axis=1)
            for target in targets
        ],
        axis=1,
    )


def level_attend(query_blocks, key_blocks, value_blocks, valid, level_index, scale):
    scores = (
        jnp.einsum("nqhd,nkhd->nhqk", query_blocks, key_blocks, preferred_element_type=jnp.float32)
        * scale
    )
    scores = jnp.where(valid[:, None, None, :], scores, -jnp.inf)
    row_peak = jnp.max(scores, axis=3, keepdims=True)
    weights = jnp.exp(scores - row_peak)
    denominator = float(1 << level_index) * jnp.sum(weights, axis=3)
    numerator = jnp.einsum(
        "nhqk,nkhd->nqhd",
        weights.astype(jnp.bfloat16),
        value_blocks,
        preferred_element_type=jnp.float32,
    )
    block_count = query_blocks.shape[0]
    row_count = query_blocks.shape[1]
    peak_rows = jnp.transpose(row_peak[..., 0], (0, 2, 1)).reshape(block_count * row_count, -1)
    denominator_rows = jnp.transpose(denominator, (0, 2, 1)).reshape(block_count * row_count, -1)
    numerator_rows = numerator.reshape(
        block_count * row_count, numerator.shape[2], numerator.shape[3]
    )
    return (peak_rows, numerator_rows, denominator_rows)


def upper_half(device_index, bit):
    return device_index // (1 << bit) % 2 == 1


def assemble_one(piece, bit_count, device_index):
    for bit in range(bit_count):
        partner = partner_2(piece, "seq", bit)
        piece = jnp.where(
            upper_half(device_index, bit),
            jnp.concatenate([partner, piece], axis=1),
            jnp.concatenate([piece, partner], axis=1),
        )
    return piece


def per_device(query_rows, key_rows, value_rows, out_weight):
    seq_count = lax.axis_size("seq")
    device_index = lax.axis_index("seq")
    token_count, head_local, head_size = query_rows.shape
    scale = float(head_size) ** (-0.5)
    top_level = seq_count.bit_length() - 1
    results = []
    local_blocks = token_count // BLOCK
    padded = with_halo(jnp.stack([key_rows, value_rows]), (("seq", 1),), BLOCK)
    padded = padded.reshape(2, local_blocks + 2, BLOCK, head_local, head_size)
    near_keys = jnp.concatenate(
        [
            padded[:, 0:local_blocks],
            padded[:, 1 : local_blocks + 1],
            padded[:, 2 : local_blocks + 2],
        ],
        axis=2,
    )
    fine_index = device_index * local_blocks + jnp.arange(local_blocks, dtype=jnp.int32)
    valid = slot_masks(fine_index, local_blocks * seq_count, 0, BLOCK)
    results.append(
        (
            0,
            level_attend(
                query_rows.reshape(local_blocks, BLOCK, head_local, head_size),
                near_keys[0],
                near_keys[1],
                valid,
                0,
                scale,
            ),
        )
    )
    half_blocks = local_blocks // 2
    first_queries = coarsen(query_rows, 1, True)
    first_pair = jnp.stack([coarsen(key_rows, 1, True), coarsen(value_rows, 1, False)])
    padded = with_halo(first_pair, (("seq", 1),), first_pair.shape[1])
    padded = padded.reshape(2, 3 * half_blocks, BLOCK, head_local, head_size)
    third_slot = jnp.stack([padded[:, 5], padded[:, 0]], axis=1)
    far_keys = jnp.concatenate([padded[:, 0:2], padded[:, 4:6], third_slot], axis=2)
    first_index = device_index * half_blocks + jnp.arange(half_blocks, dtype=jnp.int32)
    valid = slot_masks(first_index, half_blocks * seq_count, 1, BLOCK)
    results.append(
        (
            1,
            level_attend(
                first_queries.reshape(half_blocks, BLOCK, head_local, head_size),
                far_keys[0],
                far_keys[1],
                valid,
                1,
                scale,
            ),
        )
    )
    queries_at = {}
    pieces = {}
    for level_index in range(2, top_level + 1):
        queries_at[level_index] = coarsen(query_rows, level_index, True)
        pieces[level_index] = jnp.stack(
            [coarsen(key_rows, level_index, True), coarsen(value_rows, level_index, False)]
        )
    shift_levels = list(range(2, top_level + 1))
    assembled = {}
    for level_index in shift_levels:
        assembled[level_index] = assemble_one(pieces[level_index], level_index - 2, device_index)
    for level_index in shift_levels:
        group = 1 << level_index - 2
        whole_block = assembled[level_index]
        before_two = shifted(whole_block, "seq", 2 * group)
        after_two = shifted(whole_block, "seq", -2 * group)
        block_index = device_index // group
        outgoing = jnp.where(block_index % 2 == 0, before_two, after_two)
        third_block = partner_2(outgoing, "seq", level_index - 2)
        level_keys = jnp.concatenate([before_two, after_two, third_block], axis=1)[:, None]
        valid = slot_masks(jnp.reshape(block_index, (1,)), seq_count // group, level_index, BLOCK)
        results.append(
            (
                level_index,
                level_attend(
                    queries_at[level_index][None],
                    level_keys[0],
                    level_keys[1],
                    valid,
                    level_index,
                    scale,
                ),
            )
        )
    expanded = []
    for level_index, terms in results:
        factor = 1 << level_index
        expanded.append(
            (
                jnp.repeat(terms[0], factor, axis=0),
                jnp.repeat(terms[1], factor, axis=0),
                jnp.repeat(terms[2], factor, axis=0),
            )
        )
    overall = expanded[0][0]
    for entry in expanded[1:]:
        overall = jnp.maximum(overall, entry[0])
    weighted = jnp.zeros((token_count, head_local, head_size), jnp.float32)
    total_weight = jnp.zeros((token_count, head_local), jnp.float32)
    for part_peak, numerator, denominator in expanded:
        level_factor = jnp.exp(part_peak - overall)
        weighted = weighted + level_factor[:, :, None] * numerator
        total_weight = total_weight + level_factor * denominator
    attended = (weighted / total_weight[:, :, None]).astype(jnp.bfloat16)
    flattened = attended.reshape(token_count, head_local * head_size)
    weight_flat = out_weight.reshape(head_local * head_size, out_weight.shape[2])
    partial_value = jnp.dot(flattened, weight_flat, preferred_element_type=jnp.float32)
    return lax.psum_scatter(
        partial_value.astype(jnp.bfloat16), "head", scatter_dimension=1, tiled=True
    )


def solution(mesh):
    return jax.shard_map(
        per_device,
        mesh=mesh,
        in_specs=(
            P("seq", "head", None),
            P("seq", "head", None),
            P("seq", "head", None),
            P("head", None, None),
        ),
        out_specs=P("seq", "head"),
        check_vma=False,
    )
```

profile of v0, /device:TPU:11, one launch (start us, length us, event | category | flops | bytes accessed | tf_op | source)
XLA Modules:
  0.0 152.1 jit_solution(11798310255644020981)
XLA Ops:
  6.5 1.4 bitcast_reduce_fusion.1
  8.0 1.3 bitcast_reduce_fusion.2
  12.0 1.2 collective-permute-start.7
  13.9 0.7 pad_maximum_fusion.6
  14.7 3.0 %collective-permute-start.5 = (bf16[2,128,4,128]{3,1,2,0:T(8,128)(2,1)}, bf16[2,128,4,128]{3,1,2,0:T(8,128)(2,1)}, u32[]{:S(2)}, u32[]{:S(2)}) collective-permute-start(bf16[2,128,4,128]{3,1,2,0:T(8,128)(2,1)} %pad_maximum_fusion.6), channel_id=1, source_target_pairs={{4,0},{6,2},{8,4},{10,6},{12,8},{14,10},{16,12},{18,14},{20,16},{2... | collective-permute-start | bytes 786440 | tf_op jit(solution)/shard_map/ppermute | solution.py:31
  17.9 0.8 copy-done.5
  18.7 0.8 pad_maximum_fusion.5
  19.5 2.2 %collective-permute-start = (bf16[2,128,4,128]{3,1,2,0:T(8,128)(2,1)}, bf16[2,128,4,128]{3,1,2,0:T(8,128)(2,1)}, u32[]{:S(2)}, u32[]{:S(2)}) collective-permute-start(bf16[2,128,4,128]{3,1,2,0:T(8,128)(2,1)} %get-tuple-element.20), channel_id=1, source_target_pairs={{0,2},{2,4},{4,6},{6,8},{8,10},{10,12},{12,14},{14,16},{16,18},{18... | collective-permute-start | bytes 786440 | tf_op jit(solution)/shard_map/ppermute | solution.py:22
  21.7 3.1 %collective-permute-start.1 = (bf16[2,128,4,128]{3,1,2,0:T(8,128)(2,1)}, bf16[2,128,4,128]{3,1,2,0:T(8,128)(2,1)}, u32[]{:S(2)}, u32[]{:S(2)}) collective-permute-start(bf16[2,128,4,128]{3,1,2,0:T(8,128)(2,1)} %get-tuple-element.21), channel_id=1, source_target_pairs={{2,0},{4,2},{6,4},{8,6},{10,8},{12,10},{14,12},{16,14},{18,16},{20... | collective-permute-start | bytes 786440 | tf_op jit(solution)/shard_map/ppermute | solution.py:23
  24.8 1.9 %bitcast_reduce_fusion.3 = f32[32,4,128]{2,1,0:T(4,128)} fusion(bf16[512,4,128]{2,1,0:T(4,128)(2,1)} %param.4), kind=kLoop, calls=%fused_computation.45 | loop fusion | flops 507904 | bytes 589824 | tf_op jit(solution)/shard_map/reduce_sum | solution.py:37
  26.8 1.9 %bitcast_reduce_fusion.6 = f32[64,4,128]{2,1,0:T(4,128)} fusion(bf16[512,4,128]{2,1,0:T(4,128)(2,1)} %param.4), kind=kLoop, calls=%fused_computation.48 | loop fusion | flops 491520 | bytes 655360 | tf_op jit(solution)/shard_map/reduce_sum | solution.py:37
  28.7 1.0 bitcast_reduce_fusion.9
  30.5 1.2 bitcast_reduce_fusion.11
  31.7 0.8 multiply_convert_fusion.1
  32.5 1.3 fusion.33
  34.5 1.2 pad_maximum_fusion.3
  35.9 1.6 %maximum_select_fusion.2 = bf16[2,64,4,128]{3,1,2,0:T(8,128)(2,1)} fusion(bf16[1,32,4,128]{3,1,2,0:T(8,128)(2,1)} %bitcast.268, bf16[1,32,4,128]{3,1,2,0:T(8,128)(2,1)} %copy-done.17, bf16[2,32,4,128]{3,1,2,0:T(8,128)(2,1)} %collective-permute-done.11, pred[]{:T(512)S(6)} %eq.45), kind=kLoop, calls=%fused_computation.102 | loop fusion | flops 851968 | bytes 262145 | tf_op jit(solution)/shard_map/jit(_where)/select_n | solution.py:96
  37.6 1.0 collective-permute-start.12
  40.4 2.4 %collective-permute-start.4 = (bf16[2,128,4,128]{3,1,2,0:T(8,128)(2,1)}, bf16[2,128,4,128]{3,1,2,0:T(8,128)(2,1)S(1)}, u32[]{:S(2)}, u32[]{:S(2)}) collective-permute-start(bf16[2,128,4,128]{3,1,2,0:T(8,128)(2,1)} %pad_maximum_fusion.6), channel_id=1, source_target_pairs={{0,4},{2,6},{4,8},{6,10},{8,12},{10,14},{12,16},{14,18},{16,20},{1... | collective-permute-start | bytes 786440 | tf_op jit(solution)/shard_map/ppermute | solution.py:31
  42.8 1.1 maximum_select_fusion
  43.9 4.0 %collective-permute-start.3 = (bf16[2,256,4,128]{3,2,1,0:T(4,128)(2,1)}, bf16[2,256,4,128]{3,2,1,0:T(4,128)(2,1)S(1)}, u32[]{:S(2)}, u32[]{:S(2)}) collective-permute-start(bf16[2,256,4,128]{3,2,1,0:T(4,128)(2,1)} %pad_maximum_fusion.3), channel_id=1, source_target_pairs={{2,0},{4,2},{6,4},{8,6},{10,8},{12,10},{14,12},{16,14},{18,16},{20... | collective-permute-start | bytes 1572872 | tf_op jit(solution)/shard_map/ppermute | solution.py:23
  47.8 1.2 maximum_select_fusion.1
  49.0 2.7 %collective-permute-start.2 = (bf16[2,256,4,128]{3,2,1,0:T(4,128)(2,1)}, bf16[2,256,4,128]{3,2,1,0:T(4,128)(2,1)S(1)}, u32[]{:S(2)}, u32[]{:S(2)}) collective-permute-start(bf16[2,256,4,128]{3,2,1,0:T(4,128)(2,1)} %pad_maximum_fusion.3), channel_id=1, source_target_pairs={{0,2},{2,4},{4,6},{6,8},{8,10},{10,12},{12,14},{14,16},{16,18},{18... | collective-permute-start | bytes 1572872 | tf_op jit(solution)/shard_map/ppermute | solution.py:22
  51.7 2.1 %collective-permute-start.9 = (bf16[2,128,4,128]{3,1,2,0:T(8,128)(2,1)S(1)}, bf16[2,128,4,128]{3,1,2,0:T(8,128)(2,1)S(1)}, u32[]{:S(2)}, u32[]{:S(2)}) collective-permute-start(bf16[2,128,4,128]{3,1,2,0:T(8,128)(2,1)S(1)} %maximum_select_fusion), channel_id=1, source_target_pairs={{8,0},{10,2},{12,4},{14,6},{16,8},{18,10},{20,12},{22,14},{24,16},... | collective-permute-start | bytes 786440 | tf_op jit(solution)/shard_map/ppermute | solution.py:31
  53.8 1.1 pad_maximum_fusion.1
  55.0 0.8 fusion.79
  57.2 0.8 bitcast_reduce_fusion
  58.0 1.6 %fusion.12 = f32[4,128,4,128]{3,1,2,0:T(8,128)S(1)} fusion(f32[4,4,384,128]{3,2,1,0:T(8,128)S(1)} %get-tuple-element.29, f32[4,4,128]{2,1,0:T(4,128)S(1)} %get-tuple-element.28, pred[4,384]{1,0:T(4,128)(4,1)S(1)} %pad_add_fusion, bf16[1,4,384,4,128]{4,2,1,3,0:T(8,128)(2,1)S(1)} %get-tuple-element.11), kind=kOutput, calls=%fused_computation.23 | convolution fusion | flops 204472320 | bytes 5776896 | tf_op jit(solution)/shard_map/nhqk,nkhd->nqhd/dot_general | solution.py:73
  59.5 1.4 fusion.1
  61.0 3.2 %collective-permute-start.8 = (bf16[2,128,4,128]{3,1,2,0:T(8,128)(2,1)S(1)}, bf16[2,128,4,128]{3,1,2,0:T(8,128)(2,1)S(1)}, u32[]{:S(2)}, u32[]{:S(2)}) collective-permute-start(bf16[2,128,4,128]{3,1,2,0:T(8,128)(2,1)S(1)} %maximum_select_fusion), channel_id=1, source_target_pairs={{0,8},{2,10},{4,12},{6,14},{8,16},{10,18},{12,20},{14,22},{16,24},... | collective-permute-start | bytes 786440 | tf_op jit(solution)/shard_map/ppermute | solution.py:31
  64.3 1.3 collective-permute-start.14
  65.6 1.1 broadcast_select_fusion.2
  66.7 1.7 %collective-permute-done.8 = bf16[2,128,4,128]{3,1,2,0:T(8,128)(2,1)S(1)} collective-permute-done((bf16[2,128,4,128]{3,1,2,0:T(8,128)(2,1)S(1)}, bf16[2,128,4,128]{3,1,2,0:T(8,128)(2,1)S(1)}, u32[]{:S(2)}, u32[]{:S(2)}) %collective-permute-start.8) | collective-permute-done | bytes 262176 | tf_op jit(solution)/shard_map/ppermute | solution.py:31
  68.4 4.3 %collective-permute-start.13 = (bf16[2,128,4,128]{3,1,2,0:T(8,128)(2,1)S(1)}, bf16[2,128,4,128]{3,1,2,0:T(8,128)(2,1)S(1)}, u32[]{:S(2)}, u32[]{:S(2)}) collective-permute-start(bf16[2,128,4,128]{3,1,2,0:T(8,128)(2,1)S(1)} %maximum_select_fusion.1), channel_id=1, source_target_pairs={{0,16},{2,18},{4,20},{6,22},{8,24},{10,26},{12,28},{14,30},{1,17},... | collective-permute-start | bytes 786440 | tf_op jit(solution)/shard_map/ppermute | solution.py:31
  73.3 0.8 broadcast_select_fusion.1
  74.2 8.3 %collective-permute-done.13 = bf16[2,128,4,128]{3,1,2,0:T(8,128)(2,1)S(1)} collective-permute-done((bf16[2,128,4,128]{3,1,2,0:T(8,128)(2,1)S(1)}, bf16[2,128,4,128]{3,1,2,0:T(8,128)(2,1)S(1)}, u32[]{:S(2)}, u32[]{:S(2)}) %collective-permute-start.13) | collective-permute-done | bytes 262176 | tf_op jit(solution)/shard_map/ppermute | solution.py:31
  82.4 3.0 %collective-permute-start.10 = (bf16[2,128,4,128]{3,1,2,0:T(8,128)(2,1)}, bf16[2,128,4,128]{3,1,2,0:T(8,128)(2,1)}, u32[]{:S(2)}, u32[]{:S(2)}) collective-permute-start(bf16[2,128,4,128]{3,1,2,0:T(8,128)(2,1)} %get-tuple-element.22), channel_id=1, source_target_pairs={{0,4},{2,6},{4,0},{6,2},{8,12},{10,14},{12,8},{14,10},{16,20},{18,... | collective-permute-start | bytes 786440 | tf_op jit(solution)/shard_map/ppermute | solution.py:12
  85.4 0.8 broadcast_select_fusion
  86.2 0.9 copy-done.13
  87.1 6.7 %pad_maximum_fusion.2 = bf16[2,768,4,128]{3,2,1,0:T(4,128)(2,1)S(1)} fusion(bf16[2,256,4,128]{3,2,1,0:T(4,128)(2,1)S(1)} %collective-permute-done.3, bf16[1,256,4,128]{3,2,1,0:T(4,128)(2,1)S(1)} %bitcast.260, bf16[1,256,4,128]{3,2,1,0:T(4,128)(2,1)S(1)} %copy-done.10, bf16[2,256,4,128]{3,2,1,0:T(4,128)(2,1)S(1)} %collective-permute-done.2), kind=kLoop, calls=%fused_computation.10 | loop fusion | flops 2359296 | bytes 3145728 | tf_op jit(solution)/shard_map/concatenate | solution.py:24
  94.3 0.8 copy-done.15
  96.4 0.8 copy-done.20
  97.7 1.3 convolution_bitcast_fusion
  99.5 0.8 copy.226
  100.5 0.8 reshape.566
  101.4 0.8 reshape.595
  102.2 1.9 %copy.224 = f32[2,128,4,128]{3,1,0,2:T(8,128)} copy(f32[2,128,4,128]{3,1,2,0:T(8,128)} %convolution_bitcast_fusion) | data formatting | bytes 1048576 | tf_op jit(solution)/shard_map/nhqk,nkhd->nqhd/transpose | solution.py:73
  104.2 0.8 copy.227
  105.0 1.0 broadcast_in_dim.229
  107.5 1.7 %constant_dynamic-update-slice_fusion.3 = bf16[2,384,4,128]{3,1,2,0:T(8,128)(2,1)} fusion(bf16[2,384,4,128]{3,1,2,0:T(8,128)(2,1)} %copy-done.12, bf16[2,128,4,128]{3,1,2,0:T(8,128)(2,1)} %collective-permute-done.10), kind=kLoop, calls=%fused_computation.125 | loop fusion | bytes 524288 | tf_op jit(solution)/shard_map/concatenate | solution.py:178
  109.2 1.4 fusion.83
  110.8 0.7 broadcast_in_dim.214
  111.6 1.6 %reshape.573 = f32[512,4]{0,1:T(4,128)} reshape(f32[64,8,4]{1,0,2:T(8,128)} %broadcast_in_dim.214) | data formatting | bytes 16384 | tf_op jit(solution)/shard_map/reshape | solution.py:198
  113.2 0.7 broadcast_in_dim.231
  113.9 1.6 %reshape.597 = f32[512,4]{0,1:T(4,128)} reshape(f32[64,8,4]{1,0,2:T(8,128)} %broadcast_in_dim.231) | data formatting | bytes 16384 | tf_op jit(solution)/shard_map/reshape | solution.py:200
  115.5 1.9 %convolution_bitcast_fusion.2 = f32[64,4,128]{2,0,1:T(8,128)} fusion(bf16[2,384,4,128]{3,1,2,0:T(8,128)(2,1)} %constant_dynamic-update-slice_fusion.3, f32[4,64,384]{2,1,0:T(8,128)S(1)} %get-tuple-element.37, f32[4,64]{1,0:T(4,128)S(1)} %get-tuple-element.36), kind=kOutput, calls=%fused_computation.32 | convolution fusion | flops 25362432 | bytes 918528 | tf_op jit(solution)/shard_map/nhqk,nkhd->nqhd/dot_general | solution.py:73
  117.5 1.7 %constant_dynamic-update-slice_fusion.6 = bf16[2,384,4,128]{3,1,2,0:T(8,128)(2,1)} fusion(bf16[2,384,4,128]{3,1,2,0:T(8,128)(2,1)} %copy-done.13, bf16[2,128,4,128]{3,1,2,0:T(8,128)(2,1)} %collective-permute-done.15), kind=kLoop, calls=%fused_computation.128 | loop fusion | bytes 524288 | tf_op jit(solution)/shard_map/concatenate | solution.py:178
  119.2 1.3 fusion.82
  120.5 1.9 %convolution_bitcast_fusion.3 = f32[32,4,128]{2,0,1:T(8,128)} fusion(bf16[2,384,4,128]{3,1,2,0:T(8,128)(2,1)} %constant_dynamic-update-slice_fusion.6, f32[4,32,384]{2,1,0:T(8,128)S(1)} %get-tuple-element.35, f32[4,32]{1,0:T(4,128)S(1)} %get-tuple-element.34), kind=kOutput, calls=%fused_computation.33 | convolution fusion | flops 12681216 | bytes 655872 | tf_op jit(solution)/shard_map/nhqk,nkhd->nqhd/dot_general | solution.py:73
  124.1 1.5 %reshape.599 = f32[512,4]{0,1:T(4,128)} reshape(f32[32,16,4]{1,0,2:T(8,128)} %broadcast_in_dim.232) | data formatting | bytes 16384 | tf_op jit(solution)/shard_map/reshape | solution.py:200
  125.6 0.9 fusion.62
  127.1 2.1 %fusion.20 = bf16[512,4,128]{2,0,1:T(8,128)(2,1)S(1)} fusion(f32[4,128,4,128]{3,1,0,2:T(8,128)S(1)} %copy.222, f32[512,4,128]{2,0,1:T(8,128)S(1)} %bitcast.257, f32[512,4,128]{2,0,1:T(8,128)S(1)} %bitcast.258, f32[512,4]{0,1:T(4,128)S(1)} %get-tuple-element.5, f32[32,4,128]{2,0,1:T(8,128)S(1)} %copy-done.19, f32[512,4]{0,1:T(4,128)S(1)} %get-tuple-element.9, ...), kind=kLoop, calls=%fused_computation.37 | loop fusion | flops 2883584 | bytes 3915776 | tf_op jit(solution)/shard_map/convert_element_type | solution.py:212
  129.2 2.6 %bitcast_convert_fusion = bf16[512,2048]{1,0:T(8,128)(2,1)} fusion(bf16[512,4,128]{2,0,1:T(8,128)(2,1)S(1)} %fusion.20, bf16[4,128,2048]{2,1,0:T(8,128)(2,1)S(1)} %copy-done), kind=kOutput, calls=%fused_computation | convolution fusion | flops 1074790400 | bytes 4718592 | tf_op jit(solution)/shard_map/dot_general | solution.py:215
  131.9 13.3 %reduce-scatter.2.cloned.1.call-done = bf16[512,1024]{1,0:T(8,128)(2,1)} async-done(((bf16[512,2048]{1,0:T(8,128)(2,1)}), bf16[512,1024]{1,0:T(8,128)(2,1)}) %reduce-scatter.2.cloned.1.call-update) | async-done | bytes 1048592 | tf_op jit(solution)/shard_map/reduce_scatter | solution.py:216
  (138 shorter events, 16.2 us)
Async XLA Ops:
  6.5 122.7 %copy-start = (bf16[4,128,2048]{2,1,0:T(8,128)(2,1)S(1)}, bf16[4,128,2048]{2,1,0:T(8,128)(2,1)}, u32[]{:S(2)}) copy-start(bf16[4,128,2048]{2,1,0:T(8,128)(2,1)} %param.7) | copy-start | bytes 6291460
  6.5 4.3 %copy-start.2 = (bf16[512,4,128]{2,1,0:T(4,128)(2,1)S(1)}, bf16[512,4,128]{2,1,0:T(4,128)(2,1)}, u32[]{:S(2)}) copy-start(bf16[512,4,128]{2,1,0:T(4,128)(2,1)} %param.6) | copy-start | bytes 1572868
  6.5 4.5 %copy-start.1 = (bf16[512,4,128]{2,1,0:T(4,128)(2,1)S(1)}, bf16[512,4,128]{2,1,0:T(4,128)(2,1)}, u32[]{:S(2)}) copy-start(bf16[512,4,128]{2,1,0:T(4,128)(2,1)} %param.5) | copy-start | bytes 1572868
  6.5 138.7 %reduce-scatter.2.cloned.1.call-start = ((), (), s32[]{:S(2)}) async-start(), calls=%async_computation.1 | async-start | bytes 3145728 | tf_op jit(solution)/shard_map/reduce_scatter | solution.py:216
  8.0 5.2 %copy-start.18 = (bf16[32,4,128]{2,0,1:T(8,128)(2,1)}, bf16[32,4,128]{2,0,1:T(8,128)(2,1)S(1)}, u32[]{:S(2)}) copy-start(bf16[32,4,128]{2,0,1:T(8,128)(2,1)S(1)} %copy.309) | copy-start | bytes 98308
  9.3 0.6 copy-start.17
  10.5 25.4 %collective-permute-start.11 = (bf16[2,32,4,128]{3,1,2,0:T(8,128)(2,1)}, bf16[2,32,4,128]{3,1,2,0:T(8,128)(2,1)}, u32[]{:S(2)}, u32[]{:S(2)}) collective-permute-start(bf16[2,32,4,128]{3,1,2,0:T(8,128)(2,1)} %pad_maximum_fusion.8), channel_id=1, source_target_pairs={{0,2},{2,0},{4,6},{6,4},{8,10},{10,8},{12,14},{14,12},{16,18},{18,... | collective-permute-start | bytes 196616 | tf_op jit(solution)/shard_map/ppermute | solution.py:12
  12.0 28.4 %collective-permute-start.7 = (bf16[2,64,4,128]{3,1,2,0:T(8,128)(2,1)}, bf16[2,64,4,128]{3,1,2,0:T(8,128)(2,1)}, u32[]{:S(2)}, u32[]{:S(2)}) collective-permute-start(bf16[2,64,4,128]{3,1,2,0:T(8,128)(2,1)} %pad_maximum_fusion.7), channel_id=1, source_target_pairs={{0,2},{2,0},{4,6},{6,4},{8,10},{10,8},{12,14},{14,12},{16,18},{18,... | collective-permute-start | bytes 393224 | tf_op jit(solution)/shard_map/ppermute | solution.py:12
  14.7 49.6 %collective-permute-start.5 = (bf16[2,128,4,128]{3,1,2,0:T(8,128)(2,1)}, bf16[2,128,4,128]{3,1,2,0:T(8,128)(2,1)}, u32[]{:S(2)}, u32[]{:S(2)}) collective-permute-start(bf16[2,128,4,128]{3,1,2,0:T(8,128)(2,1)} %pad_maximum_fusion.6), channel_id=1, source_target_pairs={{4,0},{6,2},{8,4},{10,6},{12,8},{14,10},{16,12},{18,14},{20,16},{2... | collective-permute-start | bytes 786440 | tf_op jit(solution)/shard_map/ppermute | solution.py:31
  17.9 0.8 copy-start.5
  17.9 1.6 %copy-start.7 = (bf16[1,512,4,128]{3,1,2,0:T(8,128)(2,1)}, bf16[1,512,4,128]{3,1,2,0:T(8,128)(2,1)S(1)}, u32[]{:S(2)}) copy-start(bf16[1,512,4,128]{3,1,2,0:T(8,128)(2,1)S(1)} %get-tuple-element.41) | copy-start | bytes 1572868
  19.5 29.5 %collective-permute-start = (bf16[2,128,4,128]{3,1,2,0:T(8,128)(2,1)}, bf16[2,128,4,128]{3,1,2,0:T(8,128)(2,1)}, u32[]{:S(2)}, u32[]{:S(2)}) collective-permute-start(bf16[2,128,4,128]{3,1,2,0:T(8,128)(2,1)} %get-tuple-element.20), channel_id=1, source_target_pairs={{0,2},{2,4},{4,6},{6,8},{8,10},{10,12},{12,14},{14,16},{16,18},{18... | collective-permute-start | bytes 786440 | tf_op jit(solution)/shard_map/ppermute | solution.py:22
  21.7 30.0 %collective-permute-start.1 = (bf16[2,128,4,128]{3,1,2,0:T(8,128)(2,1)}, bf16[2,128,4,128]{3,1,2,0:T(8,128)(2,1)}, u32[]{:S(2)}, u32[]{:S(2)}) collective-permute-start(bf16[2,128,4,128]{3,1,2,0:T(8,128)(2,1)} %get-tuple-element.21), channel_id=1, source_target_pairs={{2,0},{4,2},{6,4},{8,6},{10,8},{12,10},{14,12},{16,14},{18,16},{20... | collective-permute-start | bytes 786440 | tf_op jit(solution)/shard_map/ppermute | solution.py:23
  24.8 3.9 %copy-start.3 = (bf16[512,4,128]{2,1,0:T(4,128)(2,1)S(1)}, bf16[512,4,128]{2,1,0:T(4,128)(2,1)}, u32[]{:S(2)}) copy-start(bf16[512,4,128]{2,1,0:T(4,128)(2,1)} %param.4) | copy-start | bytes 1572868
  32.5 21.3 %copy-start.6 = (bf16[1,512,4,128]{3,1,2,0:T(8,128)(2,1)S(1)}, bf16[1,512,4,128]{3,1,2,0:T(8,128)(2,1)}, u32[]{:S(2)}) copy-start(bf16[1,512,4,128]{3,1,2,0:T(8,128)(2,1)} %copy-done.5) | copy-start | bytes 1572868
  32.5 21.3 %copy-start.8 = (bf16[1,512,4,128]{3,1,2,0:T(8,128)(2,1)S(1)}, bf16[1,512,4,128]{3,1,2,0:T(8,128)(2,1)}, u32[]{:S(2)}) copy-start(bf16[1,512,4,128]{3,1,2,0:T(8,128)(2,1)} %copy-done.7) | copy-start | bytes 1572868
  33.8 0.7 copy-start.9
  37.6 6.3 %collective-permute-start.12 = (bf16[2,64,4,128]{3,1,2,0:T(8,128)(2,1)}, bf16[2,64,4,128]{3,1,2,0:T(8,128)(2,1)}, u32[]{:S(2)}, u32[]{:S(2)}) collective-permute-start(bf16[2,64,4,128]{3,1,2,0:T(8,128)(2,1)} %maximum_select_fusion.2), channel_id=1, source_target_pairs={{0,4},{2,6},{4,0},{6,2},{8,12},{10,14},{12,8},{14,10},{16,20},{18,... | collective-permute-start | bytes 393224 | tf_op jit(solution)/shard_map/ppermute | solution.py:12
  40.4 20.5 %collective-permute-start.4 = (bf16[2,128,4,128]{3,1,2,0:T(8,128)(2,1)}, bf16[2,128,4,128]{3,1,2,0:T(8,128)(2,1)S(1)}, u32[]{:S(2)}, u32[]{:S(2)}) collective-permute-start(bf16[2,128,4,128]{3,1,2,0:T(8,128)(2,1)} %pad_maximum_fusion.6), channel_id=1, source_target_pairs={{0,4},{2,6},{4,8},{6,10},{8,12},{10,14},{12,16},{14,18},{16,20},{1... | collective-permute-start | bytes 786440 | tf_op jit(solution)/shard_map/ppermute | solution.py:31
  43.9 42.4 %collective-permute-start.3 = (bf16[2,256,4,128]{3,2,1,0:T(4,128)(2,1)}, bf16[2,256,4,128]{3,2,1,0:T(4,128)(2,1)S(1)}, u32[]{:S(2)}, u32[]{:S(2)}) collective-permute-start(bf16[2,256,4,128]{3,2,1,0:T(4,128)(2,1)} %pad_maximum_fusion.3), channel_id=1, source_target_pairs={{2,0},{4,2},{6,4},{8,6},{10,8},{12,10},{14,12},{16,14},{18,16},{20... | collective-permute-start | bytes 1572872 | tf_op jit(solution)/shard_map/ppermute | solution.py:23
  49.0 38.1 %collective-permute-start.2 = (bf16[2,256,4,128]{3,2,1,0:T(4,128)(2,1)}, bf16[2,256,4,128]{3,2,1,0:T(4,128)(2,1)S(1)}, u32[]{:S(2)}, u32[]{:S(2)}) collective-permute-start(bf16[2,256,4,128]{3,2,1,0:T(4,128)(2,1)} %pad_maximum_fusion.3), channel_id=1, source_target_pairs={{0,2},{2,4},{4,6},{6,8},{8,10},{10,12},{12,14},{14,16},{16,18},{18... | collective-permute-start | bytes 1572872 | tf_op jit(solution)/shard_map/ppermute | solution.py:22
  51.7 21.0 %collective-permute-start.9 = (bf16[2,128,4,128]{3,1,2,0:T(8,128)(2,1)S(1)}, bf16[2,128,4,128]{3,1,2,0:T(8,128)(2,1)S(1)}, u32[]{:S(2)}, u32[]{:S(2)}) collective-permute-start(bf16[2,128,4,128]{3,1,2,0:T(8,128)(2,1)S(1)} %maximum_select_fusion), channel_id=1, source_target_pairs={{8,0},{10,2},{12,4},{14,6},{16,8},{18,10},{20,12},{22,14},{24,16},... | collective-permute-start | bytes 786440 | tf_op jit(solution)/shard_map/ppermute | solution.py:31
  56.1 1.0 copy-start.4
  61.0 7.4 %collective-permute-start.8 = (bf16[2,128,4,128]{3,1,2,0:T(8,128)(2,1)S(1)}, bf16[2,128,4,128]{3,1,2,0:T(8,128)(2,1)S(1)}, u32[]{:S(2)}, u32[]{:S(2)}) collective-permute-start(bf16[2,128,4,128]{3,1,2,0:T(8,128)(2,1)S(1)} %maximum_select_fusion), channel_id=1, source_target_pairs={{0,8},{2,10},{4,12},{6,14},{8,16},{10,18},{12,20},{14,22},{16,24},... | collective-permute-start | bytes 786440 | tf_op jit(solution)/shard_map/ppermute | solution.py:31
  64.3 21.1 %collective-permute-start.14 = (bf16[2,128,4,128]{3,1,2,0:T(8,128)(2,1)S(1)}, bf16[2,128,4,128]{3,1,2,0:T(8,128)(2,1)S(1)}, u32[]{:S(2)}, u32[]{:S(2)}) collective-permute-start(bf16[2,128,4,128]{3,1,2,0:T(8,128)(2,1)S(1)} %maximum_select_fusion.1), channel_id=1, source_target_pairs={{16,0},{18,2},{20,4},{22,6},{24,8},{26,10},{28,12},{30,14},{17,1},... | collective-permute-start | bytes 786440 | tf_op jit(solution)/shard_map/ppermute | solution.py:31
  66.7 20.4 %copy-start.10 = (bf16[1,256,4,128]{3,2,1,0:T(4,128)(2,1)S(1)}, bf16[1,256,4,128]{3,2,1,0:T(4,128)(2,1)}, u32[]{:S(2)}) copy-start(bf16[1,256,4,128]{3,2,1,0:T(4,128)(2,1)} %copy-done.9) | copy-start | bytes 786436
  68.4 14.0 %collective-permute-start.13 = (bf16[2,128,4,128]{3,1,2,0:T(8,128)(2,1)S(1)}, bf16[2,128,4,128]{3,1,2,0:T(8,128)(2,1)S(1)}, u32[]{:S(2)}, u32[]{:S(2)}) collective-permute-start(bf16[2,128,4,128]{3,1,2,0:T(8,128)(2,1)S(1)} %maximum_select_fusion.1), channel_id=1, source_target_pairs={{0,16},{2,18},{4,20},{6,22},{8,24},{10,26},{12,28},{14,30},{1,17},... | collective-permute-start | bytes 786440 | tf_op jit(solution)/shard_map/ppermute | solution.py:31
  72.7 21.6 %collective-permute-start.6 = (bf16[2,128,4,128]{3,1,2,0:T(8,128)(2,1)S(1)}, bf16[2,128,4,128]{3,1,2,0:T(8,128)(2,1)S(1)}, u32[]{:S(2)}, u32[]{:S(2)}) collective-permute-start(bf16[2,128,4,128]{3,1,2,0:T(8,128)(2,1)S(1)} %get-tuple-element.26), channel_id=1, source_target_pairs={{0,2},{2,0},{4,6},{6,4},{8,10},{10,8},{12,14},{14,12},{16,18},{18,... | collective-permute-start | bytes 786440 | tf_op jit(solution)/shard_map/ppermute | solution.py:12
  74.2 12.1 %copy-start.12 = (bf16[2,384,4,128]{3,1,2,0:T(8,128)(2,1)}, bf16[2,384,4,128]{3,1,2,0:T(8,128)(2,1)S(1)}, u32[]{:S(2)}) copy-start(bf16[2,384,4,128]{3,1,2,0:T(8,128)(2,1)S(1)} %get-tuple-element.23) | copy-start | bytes 2359300
  82.4 25.1 %collective-permute-start.10 = (bf16[2,128,4,128]{3,1,2,0:T(8,128)(2,1)}, bf16[2,128,4,128]{3,1,2,0:T(8,128)(2,1)}, u32[]{:S(2)}, u32[]{:S(2)}) collective-permute-start(bf16[2,128,4,128]{3,1,2,0:T(8,128)(2,1)} %get-tuple-element.22), channel_id=1, source_target_pairs={{0,4},{2,6},{4,0},{6,2},{8,12},{10,14},{12,8},{14,10},{16,20},{18,... | collective-permute-start | bytes 786440 | tf_op jit(solution)/shard_map/ppermute | solution.py:12
  86.2 0.9 copy-start.13
  86.2 31.2 %collective-permute-start.15 = (bf16[2,128,4,128]{3,1,2,0:T(8,128)(2,1)}, bf16[2,128,4,128]{3,1,2,0:T(8,128)(2,1)}, u32[]{:S(2)}, u32[]{:S(2)}) collective-permute-start(bf16[2,128,4,128]{3,1,2,0:T(8,128)(2,1)} %get-tuple-element.24), channel_id=1, source_target_pairs={{0,8},{2,10},{4,12},{6,14},{8,0},{10,2},{12,4},{14,6},{16,24},{18,... | collective-permute-start | bytes 786440 | tf_op jit(solution)/shard_map/ppermute | solution.py:12
  94.1 1.0 copy-start.15
  96.2 1.0 copy-start.20
  117.4 9.1 %copy-start.14 = (f32[128,4,128]{2,0,1:T(8,128)S(1)}, f32[128,4,128]{2,0,1:T(8,128)}, u32[]{:S(2)}) copy-start(f32[128,4,128]{2,0,1:T(8,128)} %copy.226) | copy-start | bytes 786436
  123.4 3.8 %copy-start.16 = (f32[64,4,128]{2,0,1:T(8,128)S(1)}, f32[64,4,128]{2,0,1:T(8,128)}, u32[]{:S(2)}) copy-start(f32[64,4,128]{2,0,1:T(8,128)} %convolution_bitcast_fusion.2) | copy-start | bytes 393220
  125.6 1.1 copy-start.11
  125.6 1.5 %copy-start.19 = (f32[32,4,128]{2,0,1:T(8,128)S(1)}, f32[32,4,128]{2,0,1:T(8,128)}, u32[]{:S(2)}) copy-start(f32[32,4,128]{2,0,1:T(8,128)} %convolution_bitcast_fusion.3) | copy-start | bytes 196612
Sparse Core Ops, SparseCore 0:
  132.0 13.1 reduce-scatter.1
where the time goes:
time: 154 us; the launch traced here: 152 us
  other arithmetic  38.7 us (25%)
  starting transfers between devices  34.2 us (22%)
  local copies, waits for them, and re-layouts  27.3 us (18%)
  waiting for transfers between devices  23.3 us (15%)
  between operations  14.4 us (9%)
  matrix products  14.2 us (9%)
    ppermute x6, starting transfers between devices, shifted(): lax.ppermute(value, axis, [(source, source + steps) for source in range(i...  16.2 us
    reduce_scatter x1, waiting for transfers between devices, per_device(): lax.psum_scatter(partial_value.astype(jnp.bfloat16), 'head', scatter_dime...  13.3 us
    reduce_sum x12, other arithmetic, coarsen(): summed = jnp.sum(grouped, axis=1)  10.7 us
    ppermute x6, waiting for transfers between devices, shifted(): lax.ppermute(value, axis, [(source, source + steps) for source in range(i...  9.96 us
    concatenate x2, other arithmetic, with_halo(): value = jnp.concatenate([before, value, after], axis=dim)  7.88 us
    dot_general x5, matrix products, level_attend(): jnp.einsum('nhqk,nkhd->nqhd', weights.astype(jnp.bfloat16), value_blocks,...  7.08 us
    ppermute x2, starting transfers between devices, with_halo(): after = lax.ppermute(initial, axis, down)  7.02 us
    ppermute x6, starting transfers between devices, partner_2(): return lax.ppermute(value, axis, pairs)  6.08 us
  transfers between devices with their start and end apart: 17, of which 3 were waited for; matrix products, arithmetic and copies ran while one was open for 38% of the time, Pallas kernels for 0%

commit v1 on v0

v1 whole, which is shorter than its diff:
```python
import functools

import jax
import jax.numpy as jnp
from jax import lax
from jax.experimental import pallas as pl
from jax.experimental.pallas import tpu as pltpu
from jax.sharding import PartitionSpec as P

BLOCK = 128


def partner_2(value, axis, distance):
    mask = 2**distance
    pairs = [(source, source ^ mask) for source in range(lax.axis_size(axis))]
    return lax.ppermute(value, axis, pairs)


def shifted(value, axis, steps):
    count = lax.axis_size(axis)
    initial, last = (max(0, -steps), min(count, count - steps))
    return lax.ppermute(value, axis, [(source, source + steps) for source in range(initial, last)])


def coarsen(source, level_index, average):
    count = source.shape[0] >> level_index
    grouped = source.astype(jnp.float32).reshape((count, 1 << level_index) + source.shape[1:])
    summed = jnp.sum(grouped, axis=1)
    if average:
        summed = summed / float(1 << level_index)
    return summed.astype(jnp.bfloat16)


def slot_targets(block_index, level_index):
    if level_index == 0:
        return [block_index - 1, block_index, block_index + 1]
    return [
        block_index - 2,
        block_index + 2,
        jnp.where(block_index % 2 == 0, block_index + 3, block_index - 3),
    ]


def slot_masks(block_index, block_total, level_index, width):
    targets = slot_targets(block_index, level_index)
    return jnp.concatenate(
        [
            jnp.repeat(((target >= 0) & (target < block_total))[:, None], width, axis=1)
            for target in targets
        ],
        axis=1,
    )


def level_attend(query_blocks, key_blocks, value_blocks, valid, level_index, scale):
    scores = (
        jnp.einsum("nqhd,nkhd->nhqk", query_blocks, key_blocks, preferred_element_type=jnp.float32)
        * scale
    )
    scores = jnp.where(valid[:, None, None, :], scores, -jnp.inf)
    row_peak = jnp.max(scores, axis=3, keepdims=True)
    weights = jnp.exp(scores - row_peak)
    denominator = float(1 << level_index) * jnp.sum(weights, axis=3)
    numerator = jnp.einsum(
        "nhqk,nkhd->nqhd",
        weights.astype(jnp.bfloat16),
        value_blocks,
        preferred_element_type=jnp.float32,
    )
    block_count = query_blocks.shape[0]
    row_count = query_blocks.shape[1]
    peak_rows = jnp.transpose(row_peak[..., 0], (0, 2, 1)).reshape(block_count * row_count, -1)
    denominator_rows = jnp.transpose(denominator, (0, 2, 1)).reshape(block_count * row_count, -1)
    numerator_rows = numerator.reshape(
        block_count * row_count, numerator.shape[2], numerator.shape[3]
    )
    return (peak_rows, numerator_rows, denominator_rows)


def upper_half(device_index, bit):
    return device_index // (1 << bit) % 2 == 1


def assemble_one(piece, bit_count, device_index):
    for bit in range(bit_count):
        partner = partner_2(piece, "seq", bit)
        piece = jnp.where(
            upper_half(device_index, bit),
            jnp.concatenate([partner, piece], axis=1),
            jnp.concatenate([piece, partner], axis=1),
        )
    return piece


MESH = pl.DeviceIdType.MESH
NEG = -1e30
KERNEL_TOP = 4


def spread(level):
    return 1 << (level - 2)


def layer_kernel(seq_count, levels, extra, *refs):
    q_hbm, kv_hbm, w_hbm = refs[:3]
    refs = refs[3:]
    if extra:
        xm_ref, xn_ref, xr_ref = refs[:3]
        refs = refs[3:]
    out_ref = refs[0]
    q0, kv0, w, own, qc, far, att, peak, num, den, tm, tn, tr, psend, precv = refs[1:16]
    load_sem, send_sem, recv_sem, psend_sem, precv_sem = refs[16:]
    tokens, width = q_hbm.shape
    heads = width // BLOCK
    blocks = tokens // BLOCK
    half = out_ref.shape[1]
    scale = float(BLOCK) ** (-0.5)
    s = lax.axis_index("seq")
    h = lax.axis_index("head")
    other = 1 - h

    row_count = [tokens >> level for level in range(levels + 1)]
    start_row = [sum(row_count[1:level]) for level in range(levels + 1)]
    term_row = [sum(row_count[:level]) for level in range(levels + 1)]

    load_kv = pltpu.make_async_copy(kv_hbm, kv0.at[pl.ds(BLOCK, tokens)], load_sem.at[0])
    load_q = pltpu.make_async_copy(q_hbm, q0, load_sem.at[1])
    load_w = pltpu.make_async_copy(w_hbm, w, load_sem.at[2])
    load_kv.start()
    load_q.start()
    load_w.start()

    sends = {level: [] for level in range(levels + 1)}
    arrivals = {level: [] for level in range(levels + 1)}
    greet = []
    left_ok, right_ok = s >= 1, s + 1 < seq_count
    greet += [(left_ok, s - 1), (right_ok, s + 1)]
    sends[0] += [
        (right_ok, s + 1, kv_hbm.at[pl.ds(tokens - BLOCK, BLOCK)], kv0.at[pl.ds(0, BLOCK)], 0, 0),
        (left_ok, s - 1, kv_hbm.at[pl.ds(0, BLOCK)], kv0.at[pl.ds(BLOCK + tokens, BLOCK)], 1, 1),
    ]
    arrivals[0] += [(left_ok, sends[0][0][3], 0), (right_ok, sends[0][1][3], 1)]
    n1 = row_count[1]
    mine = own.at[pl.ds(0, n1)]
    sends[1] += [
        (right_ok, s + 1, mine, far.at[pl.ds(0, n1)], 2, 2),
        (left_ok, s - 1, mine, far.at[pl.ds(n1, n1)], 3, 3),
    ]
    arrivals[1] += [(left_ok, sends[1][0][3], 2), (right_ok, sends[1][1][3], 3)]
    sem = 4
    far_row = {1: 0}
    base = 2 * n1
    slot_ok = {}
    for level in range(2, levels + 1):
        far_row[level] = base
        group = spread(level)
        rows = row_count[level]
        block, place = s // group, s % group
        odd = block % 2
        total = seq_count // group
        mine = own.at[pl.ds(start_row[level], rows)]
        third = block + 3 - 6 * odd
        sources = [block - 2, block + 2, third]
        targets = [block + 2, block - 2, third]
        oks = []
        for slot in range(3):
            to_ok = (targets[slot] >= 0) & (targets[slot] < total)
            from_ok = (sources[slot] >= 0) & (sources[slot] < total)
            oks.append(from_ok)
            for peer in range(group):
                device = targets[slot] * group + peer
                landing = pl.multiple_of(base + slot * BLOCK + place * rows, rows)
                sends[level].append(
                    (to_ok, device, mine, far.at[pl.ds(landing, rows)], sem + slot * group + peer, sem + slot * group + place)
                )
                arrivals[level].append(
                    (from_ok, far.at[pl.ds(base + slot * BLOCK + peer * rows, rows)], sem + slot * group + peer)
                )
                greet.append((to_ok, device))
        slot_ok[level] = oks
        sem += 3 * group
        base += 3 * BLOCK

    barrier = pltpu.get_barrier_semaphore()
    pl.semaphore_signal(barrier, inc=1, device_id={"head": other}, device_id_type=MESH)
    greeted = jnp.int32(1)
    for ok, device in greet:
        @pl.when(ok)
        def _(device=device):
            pl.semaphore_signal(barrier, inc=1, device_id={"seq": device}, device_id_type=MESH)

        greeted = greeted + jnp.where(ok, 1, 0).astype(jnp.int32)
    pl.semaphore_wait(barrier, greeted)

    def copy_of(entry):
        ok, device, source, landing, out_sem, in_sem = entry
        return pltpu.make_async_remote_copy(
            src_ref=source, dst_ref=landing, send_sem=send_sem.at[out_sem], recv_sem=recv_sem.at[in_sem],
            device_id={"seq": device}, device_id_type=MESH,
        )

    def start_level(level):
        for entry in sends[level]:
            @pl.when(entry[0])
            def _(entry=entry):
                copy_of(entry).start()

    def wait_level(level):
        for ok, landing, in_sem in arrivals[level]:
            @pl.when(ok)
            def _(landing=landing, in_sem=in_sem):
                pltpu.make_async_remote_copy(
                    src_ref=landing, dst_ref=landing, send_sem=send_sem.at[in_sem], recv_sem=recv_sem.at[in_sem],
                    device_id={"seq": (s + 1) % seq_count}, device_id_type=MESH,
                ).wait_recv()

            @pl.when(jnp.logical_not(ok))
            def _(landing=landing):
                landing[...] = jnp.zeros(landing.shape, landing.dtype)

    start_level(0)

    chunk = 16 << levels
    load_kv.wait()

    def average(level):
        rows = chunk >> level
        position = lax.broadcasted_iota(jnp.int32, (rows, chunk), 1) >> level
        match = position == lax.broadcasted_iota(jnp.int32, (rows, chunk), 0)
        return jnp.where(match, 1.0 / (1 << level), 0.0).astype(jnp.bfloat16)

    for level in [1] + list(range(levels, 1, -1)):
        rows = chunk >> level
        matrix = average(level)
        for c in range(tokens // chunk):
            at = pl.ds(start_row[level] + c * rows, rows)
            tokens_at = pl.ds(BLOCK + c * chunk, chunk)
            own[at, 0:width] = jnp.dot(
                matrix, kv0[tokens_at, 0:width], preferred_element_type=jnp.float32
            ).astype(jnp.bfloat16)
            own[at, width : 2 * width] = (
                jnp.dot(matrix, kv0[tokens_at, width : 2 * width], preferred_element_type=jnp.float32)
                * float(1 << level)
            ).astype(jnp.bfloat16)
        start_level(level)
    load_q.wait()
    for level in range(1, levels + 1):
        rows = chunk >> level
        matrix = average(level)
        for c in range(tokens // chunk):
            qc[pl.ds(start_row[level] + c * rows, rows), :] = jnp.dot(
                matrix, q0[pl.ds(c * chunk, chunk), :], preferred_element_type=jnp.float32
            ).astype(jnp.bfloat16)

    def bias_of(oks):
        column = lax.broadcasted_iota(jnp.int32, (1, 3 * BLOCK), 1)
        b = [jnp.where(ok, 0.0, NEG).astype(jnp.float32) for ok in oks]
        return jnp.where(column < BLOCK, b[0], jnp.where(column < 2 * BLOCK, b[1], b[2]))

    def attend(level, q_ref, q_row, rows, kv_ref, pieces, bias, to_row):
        def one_head(head):
            cols = pl.ds(head * BLOCK, BLOCK)
            vcols = pl.ds(width + head * BLOCK, BLOCK)
            keys = jnp.concatenate([kv_ref[pl.ds(a, n), cols] for a, n in pieces], axis=0)
            values = jnp.concatenate([kv_ref[pl.ds(a, n), vcols] for a, n in pieces], axis=0)
            scores = lax.dot_general(
                q_ref[pl.ds(q_row, rows), cols], keys, (((1,), (1,)), ((), ())), preferred_element_type=jnp.float32
            ) * scale
            if bias is not None:
                scores = scores + bias
            top = jnp.max(scores, axis=1, keepdims=True)
            weights = jnp.exp(scores - top)
            sums = jnp.sum(weights, axis=1, keepdims=True) * float(1 << level)
            at = pl.ds(to_row, rows)
            num[at, cols] = jnp.dot(weights.astype(jnp.bfloat16), values, preferred_element_type=jnp.float32)
            peak[at, cols] = jnp.broadcast_to(top, (rows, BLOCK))
            den[at, cols] = jnp.broadcast_to(sums, (rows, BLOCK))

        for head in range(heads):
            one_head(head)

    yes = s >= 0
    for i in range(1, blocks - 1):
        attend(0, q0, i * BLOCK, BLOCK, kv0, [(i * BLOCK, 3 * BLOCK)], None, i * BLOCK)
    wait_level(0)
    last = blocks - 1
    attend(0, q0, 0, BLOCK, kv0, [(0, 3 * BLOCK)], bias_of([left_ok, yes, yes]), 0)
    attend(
        0, q0, last * BLOCK, BLOCK, kv0, [(last * BLOCK, 3 * BLOCK)], bias_of([yes, yes, right_ok]), last * BLOCK
    )
    wait_level(1)
    attend(
        1, qc, 0, BLOCK, far, [(0, BLOCK), (n1, n1)], bias_of([left_ok, right_ok, right_ok]), term_row[1]
    )
    attend(
        1, qc, BLOCK, BLOCK, far, [(0, n1), (n1 + BLOCK, BLOCK)], bias_of([left_ok, left_ok, right_ok]),
        term_row[1] + BLOCK,
    )
    for level in range(2, levels + 1):
        wait_level(level)
        attend(
            level, qc, start_row[level], row_count[level], far, [(far_row[level], 3 * BLOCK)],
            bias_of(slot_ok[level]), term_row[level],
        )

    for head in range(heads):
        cols = pl.ds(head * BLOCK, BLOCK)

        def terms(level):
            at = pl.ds(term_row[level], row_count[level])
            return peak[at, cols], num[at, cols], den[at, cols]

        def merge(a, b):
            m = jnp.maximum(a[0], b[0])
            fa, fb = jnp.exp(a[0] - m), jnp.exp(b[0] - m)
            return m, fa * a[1] + fb * b[1], fa * a[2] + fb * b[2]

        state = terms(levels)
        if extra:
            state = merge(state, (xm_ref[:, cols], xn_ref[:, cols], xr_ref[:, cols]))
        for level in range(levels - 1, -1, -1):
            n = row_count[level + 1]
            for ref, value in zip((tm, tn, tr), state):
                ref[pl.ds(0, n, 2), :] = value
                ref[pl.ds(1, n, 2), :] = value
            wide = tuple(ref[pl.ds(0, 2 * n), :] for ref in (tm, tn, tr))
            state = merge(wide, terms(level))
        att[:, cols] = (state[1] / state[2]).astype(jnp.bfloat16)

    load_w.wait()
    theirs = pl.ds(pl.multiple_of(other * half, BLOCK), half)
    ours = pl.ds(pl.multiple_of(h * half, BLOCK), half)

    def share(c):
        at = pl.ds(c * BLOCK, BLOCK)
        return pltpu.make_async_remote_copy(
            src_ref=psend.at[at], dst_ref=precv.at[at], send_sem=psend_sem.at[c], recv_sem=precv_sem.at[c],
            device_id={"head": other}, device_id_type=MESH,
        )

    for c in range(blocks):
        at = pl.ds(c * BLOCK, BLOCK)
        psend[at, :] = jnp.dot(att[at, :], w[:, theirs], preferred_element_type=jnp.float32).astype(jnp.bfloat16)
        share(c).start()
    for c in range(blocks):
        at = pl.ds(c * BLOCK, BLOCK)
        kept = jnp.dot(att[at, :], w[:, ours], preferred_element_type=jnp.float32).astype(jnp.bfloat16)
        share(c).wait_recv()
        out_ref[at, :] = (kept.astype(jnp.float32) + precv[at, :].astype(jnp.float32)).astype(jnp.bfloat16)
    for c in range(blocks):
        share(c).wait_send()
    for level in range(levels + 1):
        for entry in sends[level]:
            @pl.when(entry[0])
            def _(entry=entry):
                copy_of(entry).wait_send()


def upper_terms(query_rows, key_rows, value_rows, first, top, rows_at):
    seq_count = lax.axis_size("seq")
    device_index = lax.axis_index("seq")
    scale = float(query_rows.shape[2]) ** (-0.5)
    merged = None
    for level_index in range(first, top + 1):
        queries = coarsen(query_rows, level_index, True)
        piece = jnp.stack([coarsen(key_rows, level_index, True), coarsen(value_rows, level_index, False)])
        whole_block = assemble_one(piece, level_index - 2, device_index)
        group = 1 << level_index - 2
        before_two = shifted(whole_block, "seq", 2 * group)
        after_two = shifted(whole_block, "seq", -2 * group)
        block_index = device_index // group
        outgoing = jnp.where(block_index % 2 == 0, before_two, after_two)
        third_block = partner_2(outgoing, "seq", level_index - 2)
        level_keys = jnp.concatenate([before_two, after_two, third_block], axis=1)[:, None]
        valid = slot_masks(jnp.reshape(block_index, (1,)), seq_count // group, level_index, BLOCK)
        terms = level_attend(queries[None], level_keys[0], level_keys[1], valid, level_index, scale)
        terms = [jnp.repeat(term, rows_at // term.shape[0], axis=0) for term in terms]
        if merged is None:
            merged = terms
        else:
            m = jnp.maximum(merged[0], terms[0])
            fa, fb = jnp.exp(merged[0] - m), jnp.exp(terms[0] - m)
            merged = [
                m,
                fa[:, :, None] * merged[1] + fb[:, :, None] * terms[1],
                fa * merged[2] + fb * terms[2],
            ]
    flat = (rows_at, merged[1].shape[1] * merged[1].shape[2])
    wide = [jnp.broadcast_to(x[:, :, None], merged[1].shape).reshape(flat) for x in (merged[0], merged[2])]
    return [wide[0], merged[1].reshape(flat), wide[1]]


def per_device(query_rows, key_rows, value_rows, out_weight):
    seq_count = lax.axis_size("seq")
    tokens, heads, head_size = query_rows.shape
    width = heads * head_size
    features = out_weight.shape[2]
    half = features // lax.axis_size("head")
    top = seq_count.bit_length() - 1
    levels = min(top, KERNEL_TOP)
    extra = []
    if top > levels:
        extra = upper_terms(query_rows, key_rows, value_rows, levels + 1, top, tokens >> levels)
    queries = query_rows.reshape(tokens, width)
    pairs = jnp.concatenate([key_rows.reshape(tokens, width), value_rows.reshape(tokens, width)], axis=1)
    weight = out_weight.reshape(width, features)
    coarse = sum(tokens >> level for level in range(1, levels + 1))
    far_rows = 2 * (tokens >> 1) + 3 * BLOCK * (levels - 1)
    copies = 4 + sum(3 * spread(level) for level in range(2, levels + 1))
    blocks = tokens // BLOCK
    bf16, f32 = jnp.bfloat16, jnp.float32
    return pl.pallas_call(
        functools.partial(layer_kernel, seq_count, levels, bool(extra)),
        out_shape=jax.ShapeDtypeStruct((tokens, half), bf16),
        in_specs=[pl.BlockSpec(memory_space=pl.ANY)] * 3 + [pl.BlockSpec(memory_space=pltpu.VMEM)] * len(extra),
        out_specs=pl.BlockSpec(memory_space=pltpu.VMEM),
        scratch_shapes=[
            pltpu.VMEM((tokens, width), bf16),
            pltpu.VMEM((tokens + 2 * BLOCK, 2 * width), bf16),
            pltpu.VMEM((width, features), bf16),
            pltpu.VMEM((coarse, 2 * width), bf16),
            pltpu.VMEM((coarse, width), bf16),
            pltpu.VMEM((far_rows, 2 * width), bf16),
            pltpu.VMEM((tokens, width), bf16),
            pltpu.VMEM((tokens + coarse, width), f32),
            pltpu.VMEM((tokens + coarse, width), f32),
            pltpu.VMEM((tokens + coarse, width), f32),
            pltpu.VMEM((tokens, BLOCK), f32),
            pltpu.VMEM((tokens, BLOCK), f32),
            pltpu.VMEM((tokens, BLOCK), f32),
            pltpu.VMEM((tokens, half), bf16),
            pltpu.VMEM((tokens, half), bf16),
            pltpu.SemaphoreType.DMA((3,)),
            pltpu.SemaphoreType.DMA((copies,)),
            pltpu.SemaphoreType.DMA((copies,)),
            pltpu.SemaphoreType.DMA((blocks,)),
            pltpu.SemaphoreType.DMA((blocks,)),
        ],
        compiler_params=pltpu.CompilerParams(
            collective_id=0, has_side_effects=True, vmem_limit_bytes=48 * 2**20
        ),
        cost_estimate=pl.CostEstimate(flops=3 * 10**9, bytes_accessed=6 * 2**20, transcendentals=2 * 10**6),
    )(queries, pairs, weight, *extra)


def solution(mesh):
    return jax.shard_map(
        per_device,
        mesh=mesh,
        in_specs=(
            P("seq", "head", None),
            P("seq", "head", None),
            P("seq", "head", None),
            P("head", None, None),
        ),
        out_specs=P("seq", "head"),
        check_vma=False,
    )
```

time: 154 us -> 77.3 us (0.50); the launches traced: 152 us -> 77.1 us
  Pallas kernels: 0 us -> 73.1 us
  other arithmetic: 38.7 us -> 0.12 us
  starting transfers between devices: 34.2 us -> 0 us
  local copies, waits for them, and re-layouts: 27.3 us -> 3.87 us
  waiting for transfers between devices: 23.3 us -> 0 us
  between operations: 14.4 us -> 0.03 us
  matrix products: 14.2 us -> 0 us
    pallas_call x0 -> x1, Pallas kernels: none -> 73.1 us  [per_device(): pl.pallas_call(functools.partial(layer_kernel, seq_count, levels, bool(ex...]
    ppermute x16 -> x0, starting transfers between devices: 34.2 us -> none  [the longest x6 16.2 us: shifted(): lax.ppermute(value, axis, [(source, source + steps) for source in range(i...]
    dot_general x11 -> x0, matrix products: 14.2 us -> none  [the longest x5 7.08 us: level_attend(): jnp.einsum('nhqk,nkhd->nqhd', weights.astype(jnp.bfloat16), value_blocks,...]
    reduce_scatter x1 -> x0, waiting for transfers between devices: 13.3 us -> none  [per_device(): lax.psum_scatter(partial_value.astype(jnp.bfloat16), 'head', scatter_dime...]
    reduce_sum x17 -> x0, other arithmetic: 13.3 us -> none  [the longest x12 10.7 us: coarsen(): summed = jnp.sum(grouped, axis=1)]
    ppermute x16 -> x0, waiting for transfers between devices: 9.99 us -> none  [the longest x6 9.96 us: shifted(): lax.ppermute(value, axis, [(source, source + steps) for source in range(i...]
    concatenate x9 -> x1, other arithmetic: 9.64 us -> 0.12 us  [per_device(): jnp.concatenate([key_rows.reshape(tokens, width), value_rows.reshape(toke...]
    reshape x17 -> x1, local copies, waits for them, and re-layouts: 10.6 us -> 1.5 us  [per_device(): value_rows.reshape(tokens, width)]
  transfers between devices with their start and end apart: 17 -> 0, of which waited for: 3 -> 0; matrix products, arithmetic and copies ran while one was open for 38% -> 0% of each run, Pallas kernels for 0% -> 0%
where the time goes in v1:
time: 77.3 us; the launch traced here: 77.1 us
  Pallas kernels  73.1 us (95%)
  local copies, waits for them, and re-layouts  3.87 us (5%)
    pallas_call x1, Pallas kernels, per_device(): pl.pallas_call(functools.partial(layer_kernel, seq_count, levels, bool(ex...  73.1 us
    unnamed x4, local copies, waits for them, and re-layouts  2.37 us

profile of v1, /device:TPU:11, one launch (start us, length us, event | category | flops | bytes accessed | tf_op | source)
XLA Modules:
  0.0 77.1 jit_solution(10244111445223567723)
XLA Ops:
  0.0 1.1 %copy.11 = bf16[64,8,4,128]{3,1,2,0:T(8,128)(2,1)S(1)} copy(bf16[64,8,4,128]{3,2,1,0:T(4,128)(2,1)} %bitcast.13) | data formatting | bytes 1048576
  1.1 0.0 copy-start
  1.1 1.5 %copy_bitcast_fusion = (bf16[512,512]{1,0:T(8,128)(2,1)S(1)}, bf16[512,512]{1,0:T(8,128)(2,1)S(1)}) fusion(bf16[64,8,4,128]{3,2,1,0:T(4,128)(2,1)} %bitcast.14, bf16[64,8,4,128]{3,2,1,0:T(4,128)(2,1)} %bitcast.15), kind=kLoop, calls=%fused_computation.1 | loop fusion | bytes 2097152 | tf_op jit(solution)/shard_map/reshape | solution.py:405
  2.6 0.1 pad_maximum_fusion.refs_1_
  2.8 0.3 copy-done
  3.0 73.1 %shard_map.46 = bf16[512,1024]{1,0:T(8,128)(2,1)S(1)} custom-call(bf16[512,512]{1,0:T(8,128)(2,1)S(1)} %bitcast.11, bf16[512,1024]{1,0:T(8,128)(2,1)S(1)} %pad_maximum_fusion.refs_1_, bf16[512,2048]{1,0:T(8,128)(2,1)S(1)} %bitcast.12), custom_call_target="tpu_custom_call" | custom-call | flops 3000000000 | bytes 6291456 | tf_op jit(solution)/shard_map/pallas_call | solution.py:412
  76.2 1.0 %copy.13 = bf16[512,1024]{1,0:T(8,128)(2,1)} copy(bf16[512,1024]{1,0:T(8,128)(2,1)S(1)} %shard_map.46) | data formatting | bytes 2097152
Async XLA Ops:
  1.1 1.9 %copy-start = (bf16[4,128,2048]{2,1,0:T(8,128)(2,1)S(1)}, bf16[4,128,2048]{2,1,0:T(8,128)(2,1)}, u32[]{:S(2)}) copy-start(bf16[4,128,2048]{2,1,0:T(8,128)(2,1)} %param.7) | copy-start | bytes 6291460

commit v2 on v1

--- a/solution.py
+++ b/solution.py
@@ -141,14 +141,17 @@
     ]
     arrivals[0] += [(left_ok, sends[0][0][3], 0), (right_ok, sends[0][1][3], 1)]
     n1 = row_count[1]
-    mine = own.at[pl.ds(0, n1)]
+    edge = BLOCK // 2
     sends[1] += [
-        (right_ok, s + 1, mine, far.at[pl.ds(0, n1)], 2, 2),
-        (left_ok, s - 1, mine, far.at[pl.ds(n1, n1)], 3, 3),
+        (right_ok, s + 1, own.at[pl.ds(0, n1 - edge)], far.at[pl.ds(0, n1 - edge)], 2, 2),
+        (left_ok, s - 1, own.at[pl.ds(edge, n1 - edge)], far.at[pl.ds(n1 + edge, n1 - edge)], 3, 3),
     ]
     arrivals[1] += [(left_ok, sends[1][0][3], 2), (right_ok, sends[1][1][3], 3)]
     sem = 4
     far_row = {1: 0}
+    own_row = {1: 0}
+    gathers = {level: [] for level in range(2, levels + 1)}
+    gathered = {level: [] for level in range(2, levels + 1)}
     base = 2 * n1
     slot_ok = {}
     for level in range(2, levels + 1):
@@ -158,27 +161,33 @@
         block, place = s // group, s % group
         odd = block % 2
         total = seq_count // group
-        mine = own.at[pl.ds(start_row[level], rows)]
+        own_row[level] = n1 + (level - 2) * BLOCK
         third = block + 3 - 6 * odd
         sources = [block - 2, block + 2, third]
         targets = [block + 2, block - 2, third]
+
+        def piece(at, level=level, rows=rows):
+            return own.at[pl.ds(pl.multiple_of(own_row[level] + at * rows, rows), rows)]
+
+        for step in range(1, group):
+            device = block * group + (place + step) % group
+            gathers[level].append((s >= 0, device, piece(place), piece(place), sem, sem))
+            gathered[level].append((s >= 0, piece((place + group - step) % group), sem))
+            greet.append((s >= 0, device))
+            sem += 1
         oks = []
+        whole = own.at[pl.ds(own_row[level], BLOCK)]
         for slot in range(3):
             to_ok = (targets[slot] >= 0) & (targets[slot] < total)
             from_ok = (sources[slot] >= 0) & (sources[slot] < total)
             oks.append(from_ok)
-            for peer in range(group):
-                device = targets[slot] * group + peer
-                landing = pl.multiple_of(base + slot * BLOCK + place * rows, rows)
-                sends[level].append(
-                    (to_ok, device, mine, far.at[pl.ds(landing, rows)], sem + slot * group + peer, sem + slot * group + place)
-                )
-                arrivals[level].append(
-                    (from_ok, far.at[pl.ds(base + slot * BLOCK + peer * rows, rows)], sem + slot * group + peer)
-                )
-                greet.append((to_ok, device))
+            landing = far.at[pl.ds(base + slot * BLOCK, BLOCK)]
+            device = targets[slot] * group + place
+            sends[level].append((to_ok, device, whole, landing, sem, sem))
+            arrivals[level].append((from_ok, landing, sem))
+            greet.append((to_ok, device))
+            sem += 1
         slot_ok[level] = oks
-        sem += 3 * group
         base += 3 * BLOCK
 
     barrier = pltpu.get_barrier_semaphore()
@@ -199,11 +208,19 @@
             device_id={"seq": device}, device_id_type=MESH,
         )
 
-    def start_level(level):
-        for entry in sends[level]:
+    def start_all(entries):
+        for entry in entries:
             @pl.when(entry[0])
             def _(entry=entry):
                 copy_of(entry).start()
+
+    def start_whole(level):
+        for ok, landing, in_sem in gathered[level]:
+            pltpu.make_async_remote_copy(
+                src_ref=landing, dst_ref=landing, send_sem=send_sem.at[in_sem], recv_sem=recv_sem.at[in_sem],
+                device_id={"seq": (s + 1) % seq_count}, device_id_type=MESH,
+            ).wait_recv()
+        start_all(sends[level])
 
     def wait_level(level):
         for ok, landing, in_sem in arrivals[level]:
@@ -218,31 +235,40 @@
             def _(landing=landing):
                 landing[...] = jnp.zeros(landing.shape, landing.dtype)
 
-    start_level(0)
-
     chunk = 16 << levels
     load_kv.wait()
 
-    def average(level):
+    def average(level, chunk=chunk):
         rows = chunk >> level
         position = lax.broadcasted_iota(jnp.int32, (rows, chunk), 1) >> level
         match = position == lax.broadcasted_iota(jnp.int32, (rows, chunk), 0)
         return jnp.where(match, 1.0 / (1 << level), 0.0).astype(jnp.bfloat16)
 
-    for level in [1] + list(range(levels, 1, -1)):
+    def shrink(level, matrix, kv_row, count, to_ref, to_row):
+        tokens_at, at = pl.ds(kv_row, count), pl.ds(to_row, count >> level)
+        to_ref[at, 0:width] = jnp.dot(
+            matrix, kv0[tokens_at, 0:width], preferred_element_type=jnp.float32
+        ).astype(jnp.bfloat16)
+        to_ref[at, width : 2 * width] = (
+            jnp.dot(matrix, kv0[tokens_at, width : 2 * width], preferred_element_type=jnp.float32)
+            * float(1 << level)
+        ).astype(jnp.bfloat16)
+
+    for level in range(levels, 0, -1):
         rows = chunk >> level
         matrix = average(level)
+        place = s % spread(level) if level > 1 else 0
         for c in range(tokens // chunk):
-            at = pl.ds(start_row[level] + c * rows, rows)
-            tokens_at = pl.ds(BLOCK + c * chunk, chunk)
-            own[at, 0:width] = jnp.dot(
-                matrix, kv0[tokens_at, 0:width], preferred_element_type=jnp.float32
-            ).astype(jnp.bfloat16)
-            own[at, width : 2 * width] = (
-                jnp.dot(matrix, kv0[tokens_at, width : 2 * width], preferred_element_type=jnp.float32)
-                * float(1 << level)
-            ).astype(jnp.bfloat16)
-        start_level(level)
+            to_row = own_row[level] + place * row_count[level] + c * rows
+            if level > 1:
+                to_row = pl.multiple_of(to_row, rows)
+            shrink(level, matrix, BLOCK + c * chunk, chunk, own, to_row)
+        if level > 2:
+            start_all(gathers[level])
+            if level == 3:
+                start_all(sends[0])
+        else:
+            start_all(sends[level])
     load_q.wait()
     for level in range(1, levels + 1):
         rows = chunk >> level
@@ -282,6 +308,8 @@
     yes = s >= 0
     for i in range(1, blocks - 1):
         attend(0, q0, i * BLOCK, BLOCK, kv0, [(i * BLOCK, 3 * BLOCK)], None, i * BLOCK)
+    for level in range(levels, 2, -1):
+        start_whole(level)
     wait_level(0)
     last = blocks - 1
     attend(0, q0, 0, BLOCK, kv0, [(0, 3 * BLOCK)], bias_of([left_ok, yes, yes]), 0)
@@ -289,6 +317,9 @@
         0, q0, last * BLOCK, BLOCK, kv0, [(last * BLOCK, 3 * BLOCK)], bias_of([yes, yes, right_ok]), last * BLOCK
     )
     wait_level(1)
+    matrix = average(1, BLOCK)
+    shrink(1, matrix, 0, BLOCK, far, n1 - edge)
+    shrink(1, matrix, BLOCK + tokens, BLOCK, far, n1)
     attend(
         1, qc, 0, BLOCK, far, [(0, BLOCK), (n1, n1)], bias_of([left_ok, right_ok, right_ok]), term_row[1]
     )
@@ -350,7 +381,7 @@
     for c in range(blocks):
         share(c).wait_send()
     for level in range(levels + 1):
-        for entry in sends[level]:
+        for entry in gathers.get(level, []) + sends[level]:
             @pl.when(entry[0])
             def _(entry=entry):
                 copy_of(entry).wait_send()
@@ -406,7 +437,7 @@
     weight = out_weight.reshape(width, features)
     coarse = sum(tokens >> level for level in range(1, levels + 1))
     far_rows = 2 * (tokens >> 1) + 3 * BLOCK * (levels - 1)
-    copies = 4 + sum(3 * spread(level) for level in range(2, levels + 1))
+    copies = 4 + sum(2 + spread(level) for level in range(2, levels + 1))
     blocks = tokens // BLOCK
     bf16, f32 = jnp.bfloat16, jnp.float32
     return pl.pallas_call(
@@ -418,7 +449,7 @@
             pltpu.VMEM((tokens, width), bf16),
             pltpu.VMEM((tokens + 2 * BLOCK, 2 * width), bf16),
             pltpu.VMEM((width, features), bf16),
-            pltpu.VMEM((coarse, 2 * width), bf16),
+            pltpu.VMEM((tokens // 2 + BLOCK * (levels - 1), 2 * width), bf16),
             pltpu.VMEM((coarse, width), bf16),
             pltpu.VMEM((far_rows, 2 * width), bf16),
             pltpu.VMEM((tokens, width), bf16),

time: 77.3 us -> 67.3 us (0.87)
  the two profiles are of different devices: /device:TPU:11 before, /device:TPU:17 now
where the time goes in v2:
time: 67.3 us; the launch traced here: 67.1 us
  Pallas kernels  63.1 us (94%)
  local copies, waits for them, and re-layouts  3.87 us (6%)
    pallas_call x1, Pallas kernels, per_device(): pl.pallas_call(functools.partial(layer_kernel, seq_count, levels, bool(ex...  63.1 us
    unnamed x4, local copies, waits for them, and re-layouts  2.37 us
    reshape x1, local copies, waits for them, and re-layouts, per_device(): value_rows.reshape(tokens, width)  1.5 us

profile of v2, /device:TPU:17, one launch (start us, length us, event | category | flops | bytes accessed | tf_op | source)
XLA Modules:
  0.0 67.1 jit_solution(4240697501473863608)
XLA Ops:
  0.0 1.1 %copy.11 = bf16[64,8,4,128]{3,1,2,0:T(8,128)(2,1)S(1)} copy(bf16[64,8,4,128]{3,2,1,0:T(4,128)(2,1)} %bitcast.13) | data formatting | bytes 1048576
  1.1 0.0 copy-start
  1.1 1.5 %copy_bitcast_fusion = (bf16[512,512]{1,0:T(8,128)(2,1)S(1)}, bf16[512,512]{1,0:T(8,128)(2,1)S(1)}) fusion(bf16[64,8,4,128]{3,2,1,0:T(4,128)(2,1)} %bitcast.14, bf16[64,8,4,128]{3,2,1,0:T(4,128)(2,1)} %bitcast.15), kind=kLoop, calls=%fused_computation.1 | loop fusion | bytes 2097152 | tf_op jit(solution)/shard_map/reshape | solution.py:436
  2.6 0.1 pad_maximum_fusion.refs_1_
  2.8 0.3 copy-done
  3.0 63.1 %shard_map.46 = bf16[512,1024]{1,0:T(8,128)(2,1)S(1)} custom-call(bf16[512,512]{1,0:T(8,128)(2,1)S(1)} %bitcast.11, bf16[512,1024]{1,0:T(8,128)(2,1)S(1)} %pad_maximum_fusion.refs_1_, bf16[512,2048]{1,0:T(8,128)(2,1)S(1)} %bitcast.12), custom_call_target="tpu_custom_call" | custom-call | flops 3000000000 | bytes 6291456 | tf_op jit(solution)/shard_map/pallas_call | solution.py:443
  66.2 1.0 %copy.13 = bf16[512,1024]{1,0:T(8,128)(2,1)} copy(bf16[512,1024]{1,0:T(8,128)(2,1)S(1)} %shard_map.46) | data formatting | bytes 2097152
Async XLA Ops:
  1.1 1.9 %copy-start = (bf16[4,128,2048]{2,1,0:T(8,128)(2,1)S(1)}, bf16[4,128,2048]{2,1,0:T(8,128)(2,1)}, u32[]{:S(2)}) copy-start(bf16[4,128,2048]{2,1,0:T(8,128)(2,1)} %param.7) | copy-start | bytes 6291460

commit v3 on v2

--- a/solution.py
+++ b/solution.py
@@ -267,8 +267,10 @@
             start_all(gathers[level])
             if level == 3:
                 start_all(sends[0])
-        else:
+        elif level == 2:
             start_all(sends[level])
+    for level in range(levels, 2, -1):
+        start_whole(level)
     load_q.wait()
     for level in range(1, levels + 1):
         rows = chunk >> level
@@ -308,14 +310,19 @@
     yes = s >= 0
     for i in range(1, blocks - 1):
         attend(0, q0, i * BLOCK, BLOCK, kv0, [(i * BLOCK, 3 * BLOCK)], None, i * BLOCK)
-    for level in range(levels, 2, -1):
-        start_whole(level)
     wait_level(0)
+    start_all(sends[1])
     last = blocks - 1
     attend(0, q0, 0, BLOCK, kv0, [(0, 3 * BLOCK)], bias_of([left_ok, yes, yes]), 0)
     attend(
         0, q0, last * BLOCK, BLOCK, kv0, [(last * BLOCK, 3 * BLOCK)], bias_of([yes, yes, right_ok]), last * BLOCK
     )
+    for level in range(2, levels + 1):
+        wait_level(level)
+        attend(
+            level, qc, start_row[level], row_count[level], far, [(far_row[level], 3 * BLOCK)],
+            bias_of(slot_ok[level]), term_row[level],
+        )
     wait_level(1)
     matrix = average(1, BLOCK)
     shrink(1, matrix, 0, BLOCK, far, n1 - edge)
@@ -327,12 +334,6 @@
         1, qc, BLOCK, BLOCK, far, [(0, n1), (n1 + BLOCK, BLOCK)], bias_of([left_ok, left_ok, right_ok]),
         term_row[1] + BLOCK,
     )
-    for level in range(2, levels + 1):
-        wait_level(level)
-        attend(
-            level, qc, start_row[level], row_count[level], far, [(far_row[level], 3 * BLOCK)],
-            bias_of(slot_ok[level]), term_row[level],
-        )
 
     for head in range(heads):
         cols = pl.ds(head * BLOCK, BLOCK)

time: 67.3 us -> 66.4 us (0.987)
  the two profiles are of different devices: /device:TPU:17 before, /device:TPU:9 now
where the time goes in v3:
time: 66.4 us; the launch traced here: 66.2 us
  Pallas kernels  62.2 us (94%)
  local copies, waits for them, and re-layouts  3.87 us (6%)
    pallas_call x1, Pallas kernels, per_device(): pl.pallas_call(functools.partial(layer_kernel, seq_count, levels, bool(ex...  62.2 us
    unnamed x4, local copies, waits for them, and re-layouts  2.37 us
    reshape x1, local copies, waits for them, and re-layouts, per_device(): value_rows.reshape(tokens, width)  1.5 us

profile of v3, /device:TPU:9, one launch (start us, length us, event | category | flops | bytes accessed | tf_op | source)
XLA Modules:
  0.0 66.2 jit_solution(14287016604688488039)
XLA Ops:
  0.0 1.1 %copy.11 = bf16[64,8,4,128]{3,1,2,0:T(8,128)(2,1)S(1)} copy(bf16[64,8,4,128]{3,2,1,0:T(4,128)(2,1)} %bitcast.13) | data formatting | bytes 1048576
  1.1 0.0 copy-start
  1.1 1.5 %copy_bitcast_fusion = (bf16[512,512]{1,0:T(8,128)(2,1)S(1)}, bf16[512,512]{1,0:T(8,128)(2,1)S(1)}) fusion(bf16[64,8,4,128]{3,2,1,0:T(4,128)(2,1)} %bitcast.14, bf16[64,8,4,128]{3,2,1,0:T(4,128)(2,1)} %bitcast.15), kind=kLoop, calls=%fused_computation.1 | loop fusion | bytes 2097152 | tf_op jit(solution)/shard_map/reshape | solution.py:437
  2.6 0.1 pad_maximum_fusion.refs_1_
  2.8 0.3 copy-done
  3.0 62.2 %shard_map.46 = bf16[512,1024]{1,0:T(8,128)(2,1)S(1)} custom-call(bf16[512,512]{1,0:T(8,128)(2,1)S(1)} %bitcast.11, bf16[512,1024]{1,0:T(8,128)(2,1)S(1)} %pad_maximum_fusion.refs_1_, bf16[512,2048]{1,0:T(8,128)(2,1)S(1)} %bitcast.12), custom_call_target="tpu_custom_call" | custom-call | flops 3000000000 | bytes 6291456 | tf_op jit(solution)/shard_map/pallas_call | solution.py:444
  65.3 1.0 %copy.13 = bf16[512,1024]{1,0:T(8,128)(2,1)} copy(bf16[512,1024]{1,0:T(8,128)(2,1)S(1)} %shard_map.46) | data formatting | bytes 2097152
Async XLA Ops:
  1.1 1.9 %copy-start = (bf16[4,128,2048]{2,1,0:T(8,128)(2,1)S(1)}, bf16[4,128,2048]{2,1,0:T(8,128)(2,1)}, u32[]{:S(2)}) copy-start(bf16[4,128,2048]{2,1,0:T(8,128)(2,1)} %param.7) | copy-start | bytes 6291460

commit v4 on v3

--- a/solution.py
+++ b/solution.py
@@ -152,6 +152,8 @@
     own_row = {1: 0}
     gathers = {level: [] for level in range(2, levels + 1)}
     gathered = {level: [] for level in range(2, levels + 1)}
+    relays = {level: [] for level in range(2, levels + 1)}
+    relayed = {level: [] for level in range(2, levels + 1)}
     base = 2 * n1
     slot_ok = {}
     for level in range(2, levels + 1):
@@ -169,24 +171,39 @@
         def piece(at, level=level, rows=rows):
             return own.at[pl.ds(pl.multiple_of(own_row[level] + at * rows, rows), rows)]
 
-        for step in range(1, group):
-            device = block * group + (place + step) % group
-            gathers[level].append((s >= 0, device, piece(place), piece(place), sem, sem))
-            gathered[level].append((s >= 0, piece((place + group - step) % group), sem))
+        peers = [block * group + (place + step) % group for step in range(1, group)]
+        direct = group > 2
+        for step, device in enumerate(peers, 1):
             greet.append((s >= 0, device))
-            sem += 1
+            if not direct:
+                gathers[level].append((s >= 0, device, piece(place), piece(place), sem, sem))
+                gathered[level].append((s >= 0, piece((place + group - step) % group), sem))
+                sem += 1
         oks = []
         whole = own.at[pl.ds(own_row[level], BLOCK)]
         for slot in range(3):
             to_ok = (targets[slot] >= 0) & (targets[slot] < total)
             from_ok = (sources[slot] >= 0) & (sources[slot] < total)
             oks.append(from_ok)
-            landing = far.at[pl.ds(base + slot * BLOCK, BLOCK)]
             device = targets[slot] * group + place
-            sends[level].append((to_ok, device, whole, landing, sem, sem))
-            arrivals[level].append((from_ok, landing, sem))
             greet.append((to_ok, device))
+            if not direct:
+                landing = far.at[pl.ds(base + slot * BLOCK, BLOCK)]
+                sends[level].append((to_ok, device, whole, landing, sem, sem))
+                arrivals[level].append((from_ok, landing, sem))
+                sem += 1
+                continue
+
+            def part(at, first=base + slot * BLOCK, rows=rows):
+                return far.at[pl.ds(pl.multiple_of(first + at * rows, rows), rows)]
+
+            sends[level].append((to_ok, device, piece(place), part(place), sem, sem))
+            relayed[level].append((from_ok, part(place), sem))
             sem += 1
+            for step, peer in enumerate(peers, 1):
+                relays[level].append((from_ok, peer, part(place), part(place), sem, sem))
+                arrivals[level].append((from_ok, part((place + group - step) % group), sem))
+                sem += 1
         slot_ok[level] = oks
         base += 3 * BLOCK
 
@@ -223,7 +240,10 @@
         start_all(sends[level])
 
     def wait_level(level):
-        for ok, landing, in_sem in arrivals[level]:
+        wait_all(arrivals[level])
+
+    def wait_all(entries):
+        for ok, landing, in_sem in entries:
             @pl.when(ok)
             def _(landing=landing, in_sem=in_sem):
                 pltpu.make_async_remote_copy(
@@ -264,13 +284,14 @@
                 to_row = pl.multiple_of(to_row, rows)
             shrink(level, matrix, BLOCK + c * chunk, chunk, own, to_row)
         if level > 2:
-            start_all(gathers[level])
+            start_all(gathers[level] or sends[level])
             if level == 3:
                 start_all(sends[0])
         elif level == 2:
             start_all(sends[level])
     for level in range(levels, 2, -1):
-        start_whole(level)
+        if gathers[level]:
+            start_whole(level)
     load_q.wait()
     for level in range(1, levels + 1):
         rows = chunk >> level
@@ -310,6 +331,9 @@
     yes = s >= 0
     for i in range(1, blocks - 1):
         attend(0, q0, i * BLOCK, BLOCK, kv0, [(i * BLOCK, 3 * BLOCK)], None, i * BLOCK)
+    for level in range(levels, 2, -1):
+        wait_all(relayed[level])
+        start_all(relays[level])
     wait_level(0)
     start_all(sends[1])
     last = blocks - 1
@@ -323,6 +347,33 @@
             level, qc, start_row[level], row_count[level], far, [(far_row[level], 3 * BLOCK)],
             bias_of(slot_ok[level]), term_row[level],
         )
+    def terms(level, cols):
+        at = pl.ds(term_row[level], row_count[level])
+        return peak[at, cols], num[at, cols], den[at, cols]
+
+    def merge(a, b):
+        m = jnp.maximum(a[0], b[0])
+        fa, fb = jnp.exp(a[0] - m), jnp.exp(b[0] - m)
+        return m, fa * a[1] + fb * b[1], fa * a[2] + fb * b[2]
+
+    def refine(state, high, low, cols):
+        for level in range(high - 1, low - 1, -1):
+            n = row_count[level + 1]
+            for ref, value in zip((tm, tn, tr), state):
+                ref[pl.ds(0, n, 2), :] = value
+                ref[pl.ds(1, n, 2), :] = value
+            wide = tuple(ref[pl.ds(0, 2 * n), :] for ref in (tm, tn, tr))
+            state = merge(wide, terms(level, cols))
+        return state
+
+    for head in range(heads):
+        cols = pl.ds(head * BLOCK, BLOCK)
+        state = terms(levels, cols)
+        if extra:
+            state = merge(state, (xm_ref[:, cols], xn_ref[:, cols], xr_ref[:, cols]))
+        at = pl.ds(term_row[2], row_count[2])
+        peak[at, cols], num[at, cols], den[at, cols] = refine(state, levels, 2, cols)
+
     wait_level(1)
     matrix = average(1, BLOCK)
     shrink(1, matrix, 0, BLOCK, far, n1 - edge)
@@ -337,26 +388,7 @@
 
     for head in range(heads):
         cols = pl.ds(head * BLOCK, BLOCK)
-
-        def terms(level):
-            at = pl.ds(term_row[level], row_count[level])
-            return peak[at, cols], num[at, cols], den[at, cols]
-
-        def merge(a, b):
-            m = jnp.maximum(a[0], b[0])
-            fa, fb = jnp.exp(a[0] - m), jnp.exp(b[0] - m)
-            return m, fa * a[1] + fb * b[1], fa * a[2] + fb * b[2]
-
-        state = terms(levels)
-        if extra:
-            state = merge(state, (xm_ref[:, cols], xn_ref[:, cols], xr_ref[:, cols]))
-        for level in range(levels - 1, -1, -1):
-            n = row_count[level + 1]
-            for ref, value in zip((tm, tn, tr), state):
-                ref[pl.ds(0, n, 2), :] = value
-                ref[pl.ds(1, n, 2), :] = value
-            wide = tuple(ref[pl.ds(0, 2 * n), :] for ref in (tm, tn, tr))
-            state = merge(wide, terms(level))
+        state = refine(terms(2, cols), 2, 0, cols)
         att[:, cols] = (state[1] / state[2]).astype(jnp.bfloat16)
 
     load_w.wait()
@@ -382,7 +414,7 @@
     for c in range(blocks):
         share(c).wait_send()
     for level in range(levels + 1):
-        for entry in gathers.get(level, []) + sends[level]:
+        for entry in gathers.get(level, []) + relays.get(level, []) + sends[level]:
             @pl.when(entry[0])
             def _(entry=entry):
                 copy_of(entry).wait_send()
@@ -438,7 +470,7 @@
     weight = out_weight.reshape(width, features)
     coarse = sum(tokens >> level for level in range(1, levels + 1))
     far_rows = 2 * (tokens >> 1) + 3 * BLOCK * (levels - 1)
-    copies = 4 + sum(2 + spread(level) for level in range(2, levels + 1))
+    copies = 4 + sum(3 * spread(level) for level in range(2, levels + 1))
     blocks = tokens // BLOCK
     bf16, f32 = jnp.bfloat16, jnp.float32
     return pl.pallas_call(

time: 66.4 us -> 65.6 us (0.988)
  the two profiles are of different devices: /device:TPU:9 before, /device:TPU:11 now
where the time goes in v4:
time: 65.6 us; the launch traced here: 65.4 us
  Pallas kernels  61.4 us (94%)
  local copies, waits for them, and re-layouts  3.87 us (6%)
    pallas_call x1, Pallas kernels, per_device(): pl.pallas_call(functools.partial(layer_kernel, seq_count, levels, bool(ex...  61.4 us
    unnamed x4, local copies, waits for them, and re-layouts  2.37 us
    reshape x1, local copies, waits for them, and re-layouts, per_device(): value_rows.reshape(tokens, width)  1.5 us

profile of v4, /device:TPU:11, one launch (start us, length us, event | category | flops | bytes accessed | tf_op | source)
XLA Modules:
  0.0 65.4 jit_solution(11960327398705376350)
XLA Ops:
  0.0 1.1 %copy.11 = bf16[64,8,4,128]{3,1,2,0:T(8,128)(2,1)S(1)} copy(bf16[64,8,4,128]{3,2,1,0:T(4,128)(2,1)} %bitcast.13) | data formatting | bytes 1048576
  1.1 0.0 copy-start
  1.1 1.5 %copy_bitcast_fusion = (bf16[512,512]{1,0:T(8,128)(2,1)S(1)}, bf16[512,512]{1,0:T(8,128)(2,1)S(1)}) fusion(bf16[64,8,4,128]{3,2,1,0:T(4,128)(2,1)} %bitcast.14, bf16[64,8,4,128]{3,2,1,0:T(4,128)(2,1)} %bitcast.15), kind=kLoop, calls=%fused_computation.1 | loop fusion | bytes 2097152 | tf_op jit(solution)/shard_map/reshape | solution.py:469
  2.6 0.1 pad_maximum_fusion.refs_1_
  2.8 0.3 copy-done
  3.0 61.4 %shard_map.46 = bf16[512,1024]{1,0:T(8,128)(2,1)S(1)} custom-call(bf16[512,512]{1,0:T(8,128)(2,1)S(1)} %bitcast.11, bf16[512,1024]{1,0:T(8,128)(2,1)S(1)} %pad_maximum_fusion.refs_1_, bf16[512,2048]{1,0:T(8,128)(2,1)S(1)} %bitcast.12), custom_call_target="tpu_custom_call" | custom-call | flops 3000000000 | bytes 6291456 | tf_op jit(solution)/shard_map/pallas_call | solution.py:476
  64.4 1.0 %copy.13 = bf16[512,1024]{1,0:T(8,128)(2,1)} copy(bf16[512,1024]{1,0:T(8,128)(2,1)S(1)} %shard_map.46) | data formatting | bytes 2097152
Async XLA Ops:
  1.1 1.9 %copy-start = (bf16[4,128,2048]{2,1,0:T(8,128)(2,1)S(1)}, bf16[4,128,2048]{2,1,0:T(8,128)(2,1)}, u32[]{:S(2)}) copy-start(bf16[4,128,2048]{2,1,0:T(8,128)(2,1)} %param.7) | copy-start | bytes 6291460
